TPU v7x, 32 devices: a whole 2x2x4 slice. The times are simulated.
32 devices in a mesh: replica: 4 (over x, core), shard: 8 (over z, y).
Axes of the slice: x: 2, y: 2, z: 4, core: 2. Of those that a mesh axis runs over, the one named last changes fastest.
Arguments:
- tokens: bfloat16 [32, 128, 1536], P(('replica', 'shard')), may hold values from -6 to 6
- segments: int32 [32, 128], P(('replica', 'shard')), may hold values from 0 to 3, never falling along the last dimension, each value on 1 to 64 neighbouring positions
- gain_attn: bfloat16 [1536], P('shard'), may hold values from 0.25 to 1.75
- w_qkv: bfloat16 [1536, 2048], P('shard'), may hold values from -0.15625 to 0.15625
- b_qkv: bfloat16 [2048], P('shard'), may hold values from -3 to 3
- w_out: bfloat16 [1536, 1536], P('shard'), may hold values from -0.625 to 0.625
- gain_ffn: bfloat16 [1536], P('shard'), may hold values from 0.25 to 1.75
- w_gate: bfloat16 [1536, 8960], P('shard'), may hold values from -0.15625 to 0.15625
- w_up: bfloat16 [1536, 8960], P('shard'), may hold values from -0.15625 to 0.15625
- w_down: bfloat16 [8960, 1536], P('shard'), may hold values from -0.0625 to 0.0625
- cotangent: bfloat16 [32, 128, 1536], P(('replica', 'shard')), may hold values from -6 to 6
Outputs:
- out: bfloat16 [32, 128, 1536], P(('replica', 'shard'))
- grad_tokens: bfloat16 [32, 128, 1536], P(('replica', 'shard'))
- grad_gain_attn: float32 [1536], P('shard')
- grad_w_qkv: float32 [1536, 2048], P('shard')
- grad_b_qkv: float32 [2048], P('shard')
- grad_w_out: float32 [1536, 1536], P('shard')
- grad_gain_ffn: float32 [1536], P('shard')
- grad_w_gate: float32 [1536, 8960], P('shard')
- grad_w_up: float32 [1536, 8960], P('shard')
- grad_w_down: float32 [8960, 1536], P('shard')
Inputs may be any that keep to these rules, and one draw needn't show every extreme that they name: `segments`: along each sequence the document numbers never fall; a document has 1 to 64 tokens, and one of each sequence has exactly 64.
All inputs are finite; a program needn't handle non-finite values.
Results may differ from a plain program's by a relative error of at most 0.018.
Values may be sent and summed in bfloat16 or wider, within the bound.
A program may use at most 448 MiB of HBM per device.

v0:
```python
import math

import jax
import jax.numpy as jnp
from jax import lax
from jax.experimental import pallas as pl
from jax.experimental.pallas import tpu as pltpu
from jax.sharding import PartitionSpec as P

QUERY_HEADS = 12
KEY_VALUE_HEADS = 2
HEAD_DIMENSION = 128


eps_norm = 1e-06
rope_base = 1000000.0


def tables(segment_ids, head_size):
    token_length = segment_ids.shape[-1]
    row_index = jnp.arange(token_length, dtype=jnp.int32)
    earlier = jnp.sum(
        (segment_ids[..., None, :] < segment_ids[..., :, None]).astype(jnp.int32),
        axis=-1,
        dtype=jnp.int32,
    )
    positions = (row_index - earlier).astype(jnp.float32)
    frequencies = jnp.exp(
        jnp.arange(head_size // 2, dtype=jnp.float32) * (-2.0 * math.log(rope_base) / head_size)
    )
    angles = positions[..., None] * frequencies
    cosine = jnp.concatenate([jnp.cos(angles), jnp.cos(angles)], axis=-1)
    sine_vals = jnp.concatenate([jnp.sin(angles), jnp.sin(angles)], axis=-1)
    allowed = (
        (segment_ids[..., None, :] == segment_ids[..., :, None])
        & (row_index[None, :] <= row_index[:, None])
    ).astype(jnp.int32)
    return (cosine, sine_vals, allowed)


def apply_rotation(values, cosine, sine_vals):
    halfway = values.shape[-1] // 2
    turned = jnp.concatenate([-values[..., halfway:], values[..., :halfway]], axis=-1)
    return values * cosine + turned * sine_vals


def rotate_back(values, cosine, sine_vals):
    halfway = values.shape[-1] // 2
    shifted = values * sine_vals
    return values * cosine + jnp.concatenate(
        [shifted[..., halfway:], -shifted[..., :halfway]], axis=-1
    )


def norm_forward(hidden, gain_vec):
    rstd_rows = lax.rsqrt(jnp.mean(hidden * hidden, axis=-1, keepdims=True) + eps_norm)
    unit_rows = hidden * rstd_rows
    return (unit_rows * gain_vec, unit_rows, rstd_rows)


def norm_backward(grad_in, gain_vec, unit_rows, rstd_rows):
    inner_grad = grad_in * gain_vec
    return rstd_rows * (
        inner_grad - unit_rows * jnp.mean(inner_grad * unit_rows, axis=-1, keepdims=True)
    )


def column_term(left_side, right_side):
    return jnp.einsum("lf,ld->fd", left_side, right_side, preferred_element_type=jnp.float32)


def to_columns(rows):
    ranks = lax.axis_size("shard")
    depth, width = rows.shape
    split = rows.reshape(depth, ranks, width // ranks).transpose(1, 0, 2)
    return lax.all_to_all(split, "shard", 0, 0, tiled=True).reshape(ranks * depth, width // ranks)


def to_rows(columns):
    ranks, copies = lax.axis_size("shard"), lax.axis_size("replica")
    depth, width = columns.shape
    depth = depth // ranks
    parts = columns.reshape(ranks, copies, depth // copies, width)
    part = lax.psum_scatter(parts, "replica", scatter_dimension=1, tiled=False)
    part = lax.all_to_all(part, "shard", 0, 0, tiled=True)
    part = part.transpose(1, 0, 2).reshape(depth // copies, ranks * width)
    return lax.all_gather(part, "replica", axis=0, tiled=True)


def shards(
    tokens, segments, gain_attn, w_qkv, b_qkv, w_out, gain_ffn, w_gate, w_up, w_down, cotangent
):
    heads_per_group = QUERY_HEADS // KEY_VALUE_HEADS
    head_dimension = QUERY_HEADS * HEAD_DIMENSION
    key_value_limit = head_dimension + KEY_VALUE_HEADS * HEAD_DIMENSION
    logit_scale = HEAD_DIMENSION ** (-0.5)
    token_length = tokens.shape[1]
    full_gain_attn, full_qkv, full_bias, full_out, full_gain_ffn = (
        lax.all_gather(gain_attn, "shard", axis=0, tiled=True),
        lax.all_gather(w_qkv, "shard", axis=0, tiled=True),
        lax.all_gather(b_qkv, "shard", axis=0, tiled=True),
        lax.all_gather(w_out, "shard", axis=0, tiled=True),
        lax.all_gather(gain_ffn, "shard", axis=0, tiled=True),
    )
    gate_columns = to_columns(w_gate)
    up_columns = to_columns(w_up)
    all_cot = lax.all_gather(cotangent[0], "shard", axis=0, tiled=True)
    gain_first = full_gain_attn.astype(jnp.float32)
    gain_second = full_gain_ffn.astype(jnp.float32)
    cosine, sine_vals, allowed = tables(segments[0], HEAD_DIMENSION)
    cosine_per_head = cosine[:, None, :]
    sine_per_head = sine_vals[:, None, :]
    inputs = tokens[0].astype(jnp.float32)
    normed_first, unit_first, rstd_first = norm_forward(inputs, gain_first)
    acts_first = normed_first.astype(jnp.bfloat16)
    joined_projection = jnp.dot(
        acts_first, full_qkv, preferred_element_type=jnp.float32
    ) + full_bias.astype(jnp.float32)
    query_rows = apply_rotation(
        joined_projection[:, :head_dimension].reshape(token_length, QUERY_HEADS, HEAD_DIMENSION),
        cosine_per_head,
        sine_per_head,
    )
    query_reduced = (
        (query_rows * logit_scale)
        .astype(jnp.bfloat16)
        .reshape(token_length, KEY_VALUE_HEADS, heads_per_group, HEAD_DIMENSION)
    )
    k_low = apply_rotation(
        joined_projection[:, head_dimension:key_value_limit].reshape(
            token_length, KEY_VALUE_HEADS, HEAD_DIMENSION
        ),
        cosine_per_head,
        sine_per_head,
    ).astype(jnp.bfloat16)
    value_reduced = (
        joined_projection[:, key_value_limit:]
        .reshape(token_length, KEY_VALUE_HEADS, HEAD_DIMENSION)
        .astype(jnp.bfloat16)
    )
    scores = jnp.einsum("ikrd,jkd->krij", query_reduced, k_low, preferred_element_type=jnp.float32)
    scores = jnp.where(allowed != 0, scores, -1e30)
    largest = jnp.max(scores, axis=-1, keepdims=True)
    exponents = jnp.exp(scores - largest)
    soft_probs = exponents / jnp.sum(exponents, axis=-1, keepdims=True)
    soft_low = soft_probs.astype(jnp.bfloat16)
    attended = jnp.einsum(
        "krij,jkd->ikrd", soft_low, value_reduced, preferred_element_type=jnp.float32
    )
    attended = attended.reshape(token_length, head_dimension).astype(jnp.bfloat16)
    hidden_mid = inputs + jnp.dot(attended, full_out, preferred_element_type=jnp.float32)
    normed_second, unit_second, rstd_second = norm_forward(hidden_mid, gain_second)
    acts_second = normed_second.astype(jnp.bfloat16)
    all_acts = lax.all_gather(acts_second, "shard", axis=0, tiled=True)
    gate_vals = jnp.dot(all_acts, gate_columns, preferred_element_type=jnp.float32)
    up_vals = jnp.dot(all_acts, up_columns, preferred_element_type=jnp.float32)
    sigmoid_gate = jax.nn.sigmoid(gate_vals)
    active = gate_vals * sigmoid_gate
    mixed_hidden = (active * up_vals).astype(jnp.bfloat16)
    d_mixed = jnp.einsum("ld,fd->lf", all_cot, w_down, preferred_element_type=jnp.float32)
    d_active = d_mixed * up_vals
    d_gate = (
        d_active * sigmoid_gate + d_active * gate_vals * sigmoid_gate * (1.0 - sigmoid_gate)
    ).astype(jnp.bfloat16)
    d_up = (d_mixed * active).astype(jnp.bfloat16)
    d_normed_part = jnp.einsum("lf,df->ld", d_gate, gate_columns, preferred_element_type=jnp.float32)
    d_normed_part = d_normed_part + jnp.einsum(
        "lf,df->ld", d_up, up_columns, preferred_element_type=jnp.float32
    )
    d_normed_second = lax.psum_scatter(
        d_normed_part.astype(jnp.bfloat16), "shard", scatter_dimension=0, tiled=True
    ).astype(jnp.float32)
    down_part = jnp.dot(mixed_hidden, w_down, preferred_element_type=jnp.float32)
    result = (
        hidden_mid
        + lax.psum_scatter(
            down_part.astype(jnp.bfloat16), "shard", scatter_dimension=0, tiled=True
        ).astype(jnp.float32)
    ).astype(jnp.bfloat16)
    grad_out = cotangent[0]
    down_grad = column_term(mixed_hidden, all_cot).astype(jnp.bfloat16)
    gate_grad = to_rows(column_term(all_acts, d_gate).astype(jnp.bfloat16))
    up_grad = to_rows(column_term(all_acts, d_up).astype(jnp.bfloat16))
    gain_second_grad = jnp.sum(d_normed_second * unit_second, axis=0)
    d_hidden_mid = grad_out.astype(jnp.float32) + norm_backward(
        d_normed_second, gain_second, unit_second, rstd_second
    )
    d_branch = d_hidden_mid.astype(jnp.bfloat16)
    out_grad_term = jnp.einsum("le,ld->ed", attended, d_branch, preferred_element_type=jnp.float32)
    attended_gradient = jnp.einsum(
        "ld,ed->le", d_branch, full_out, preferred_element_type=jnp.float32
    )
    attended_gradient = attended_gradient.astype(jnp.bfloat16).reshape(
        token_length, KEY_VALUE_HEADS, heads_per_group, HEAD_DIMENSION
    )
    d_probs = jnp.einsum(
        "ikrd,jkd->krij", attended_gradient, value_reduced, preferred_element_type=jnp.float32
    )
    value_gradient = jnp.einsum(
        "krij,ikrd->jkd", soft_low, attended_gradient, preferred_element_type=jnp.float32
    )
    d_scores = soft_probs * (d_probs - jnp.sum(soft_probs * d_probs, axis=-1, keepdims=True))
    d_scores_low = d_scores.astype(jnp.bfloat16)
    d_queries = jnp.einsum(
        "krij,jkd->ikrd", d_scores_low, k_low, preferred_element_type=jnp.float32
    )
    d_queries = rotate_back(
        d_queries.reshape(token_length, QUERY_HEADS, HEAD_DIMENSION) * logit_scale,
        cosine_per_head,
        sine_per_head,
    )
    key_gradient = jnp.einsum(
        "krij,ikrd->jkd", d_scores_low, query_reduced, preferred_element_type=jnp.float32
    )
    key_gradient = rotate_back(key_gradient, cosine_per_head, sine_per_head)
    d_joined = jnp.concatenate(
        [
            d_queries.reshape(token_length, head_dimension),
            key_gradient.reshape(token_length, KEY_VALUE_HEADS * HEAD_DIMENSION),
            value_gradient.reshape(token_length, KEY_VALUE_HEADS * HEAD_DIMENSION),
        ],
        axis=1,
    ).astype(jnp.bfloat16)
    bias_grad_term = jnp.sum(d_joined.astype(jnp.float32), axis=0)
    qkv_grad_term = jnp.einsum(
        "ld,le->de", acts_first, d_joined, preferred_element_type=jnp.float32
    )
    d_normed_first = jnp.einsum("le,de->ld", d_joined, full_qkv, preferred_element_type=jnp.float32)
    gain_first_grad = jnp.sum(d_normed_first * unit_first, axis=0)
    d_inputs = d_hidden_mid + norm_backward(d_normed_first, gain_first, unit_first, rstd_first)
    owned = (
        lax.psum_scatter(
            gain_first_grad.astype(jnp.bfloat16), "shard", scatter_dimension=0, tiled=True
        ).astype(jnp.float32),
        lax.psum_scatter(
            qkv_grad_term.astype(jnp.bfloat16), "shard", scatter_dimension=0, tiled=True
        ).astype(jnp.float32),
        lax.psum_scatter(
            bias_grad_term.astype(jnp.bfloat16), "shard", scatter_dimension=0, tiled=True
        ).astype(jnp.float32),
        lax.psum_scatter(
            out_grad_term.astype(jnp.bfloat16), "shard", scatter_dimension=0, tiled=True
        ).astype(jnp.float32),
        lax.psum_scatter(
            gain_second_grad.astype(jnp.bfloat16), "shard", scatter_dimension=0, tiled=True
        ).astype(jnp.float32),
    )
    summed = (
        lax.psum(owned[0].astype(jnp.bfloat16), "replica").astype(jnp.float32),
        lax.psum(owned[1].astype(jnp.bfloat16), "replica").astype(jnp.float32),
        lax.psum(owned[2].astype(jnp.bfloat16), "replica").astype(jnp.float32),
        lax.psum(owned[3].astype(jnp.bfloat16), "replica").astype(jnp.float32),
        lax.psum(owned[4].astype(jnp.bfloat16), "replica").astype(jnp.float32),
        gate_grad.astype(jnp.float32),
        up_grad.astype(jnp.float32),
        lax.psum(down_grad, "replica").astype(jnp.float32),
    )
    return (
        result[None],
        d_inputs.astype(jnp.bfloat16)[None],
        summed[0],
        summed[1],
        summed[2],
        summed[3],
        summed[4],
        summed[5],
        summed[6],
        summed[7],
    )


MESH = pl.DeviceIdType.MESH
BF, F32 = jnp.bfloat16, jnp.float32
HBM = pl.BlockSpec(memory_space=pl.ANY)
VMEM = pl.BlockSpec(memory_space=pltpu.VMEM)
DMA = pltpu.SemaphoreType.DMA


def shaped(*shape, dtype=BF):
    return jax.ShapeDtypeStruct(shape, dtype)


def low(*shape):
    return pltpu.VMEM(shape, BF)


def full(*shape):
    return pltpu.VMEM(shape, F32)


def dot(a, b):
    return lax.dot_general(a, b, (((1,), (0,)), ((), ())), preferred_element_type=F32)


def dot_nt(a, b):
    return lax.dot_general(a, b, (((1,), (1,)), ((), ())), preferred_element_type=F32)


def rows_of(start, size, unit=16):
    return pl.ds(pl.multiple_of(start, unit), size)


def quarter(t, q):
    return rows_of(192 * t + 48 * q, 48)


def send(src, dst, send_sem, recv_sem, device):
    copy = pltpu.make_async_remote_copy(
        src_ref=src, dst_ref=dst, send_sem=send_sem, recv_sem=recv_sem, device_id=device, device_id_type=MESH
    )
    copy.start()


class Place:
    def __init__(self):
        self.r = r = lax.axis_index("replica")
        self.s = s = lax.axis_index("shard")
        self.x, self.c, self.z, self.y = r // 2, r % 2, s // 2, s % 2
        self.rc, self.rx, self.rd = r + 1 - 2 * self.c, (r + 2) % 4, 3 - r
        self.core, self.across, self.side = (self.rc, s), (self.rx, s), (r, s + 1 - 2 * self.y)

    def peer(self, t):
        return (self.r, t)

    def line(self, k):
        near = self.z + (1 - 2 * (self.z % 2)) * (k % 2)
        far = k + (self.z // 2) * (3 - 2 * k)
        return (1 - k // 2) * near + (k // 2) * far

    def onward(self, zz, copy):
        pl.when((zz <= self.z) & (self.z < 3))(lambda: copy(0, self.peer(self.s + 2)))
        pl.when((zz >= self.z) & (self.z > 0))(lambda: copy(1, self.peer(self.s - 2)))

    def went_onward(self, zz, wait):
        pl.when((zz <= self.z) & (self.z < 3))(lambda: wait(0))
        pl.when((zz >= self.z) & (self.z > 0))(lambda: wait(1))

    def reduce_step(self, zz, add, hand):
        pl.when((zz >= self.z) & (self.z > 0))(lambda: add(zz))
        pl.when((zz < self.z) & (self.z < 3))(lambda: add(zz))
        pl.when((zz == self.z) & (self.z < 3))(lambda: add(4))
        pl.when(zz > self.z)(lambda: hand(zz, self.peer(self.s + 2)))
        pl.when(zz < self.z - 1)(lambda: hand(zz, self.peer(self.s - 2)))
        pl.when(zz == self.z - 1)(lambda: hand(4, self.peer(self.s - 2)))

    def mine(self, zz):
        return 2 * zz + self.y

    def theirs(self, zz):
        return 2 * zz + 1 - self.y

    def greet(self, steps):
        bar = pltpu.get_barrier_semaphore()
        devices = [self.core, self.across] + [(self.r, (self.s + k) % 8) for k in steps]
        for device in devices:
            pl.semaphore_signal(bar, inc=1, device_id=device, device_id_type=MESH)
        pl.semaphore_wait(bar, len(devices))

    def arrived(self, ref, sem, spare):
        pltpu.make_async_remote_copy(
            src_ref=ref, dst_ref=ref, send_sem=spare, recv_sem=sem, device_id=self.core, device_id_type=MESH
        ).wait_recv()

    def sent(self, ref, sem, spare):
        pltpu.make_async_remote_copy(
            src_ref=ref, dst_ref=ref, send_sem=sem, recv_sem=spare, device_id=self.core, device_id_type=MESH
        ).wait_send()


def inverse_norm(v):
    return lax.rsqrt(jnp.mean(v * v, axis=-1, keepdims=True) + eps_norm)


class Gather:
    def __init__(self, p, spare, view, arrivals, along, aside):
        self.p, self.spare, self.view = p, spare, view
        self.arrivals, self.along, self.aside = arrivals, along, aside

    def move(self, src, t, zz):
        p, dst, sem = self.p, self.view(t), self.arrivals(t)
        p.onward(zz, lambda d, device: send(src, dst, self.along.at[zz, d], sem, device))
        send(src, dst, self.aside.at[zz], sem, p.side)

    def start(self, src):
        self.move(src, self.p.s, self.p.z)

    def wait(self, t):
        self.p.arrived(self.view(t), self.arrivals(t), self.spare)

    def step(self, k, then=None):
        zz = self.p.line(k)
        t = self.p.mine(zz)
        self.wait(t)
        self.move(self.view(t), t, zz)
        if then is not None:
            then(t)

    def other(self, k, then=None):
        t = self.p.theirs(self.p.line(k))
        self.wait(t)
        if then is not None:
            then(t)

    def finish(self):
        block = self.view(self.p.s)
        for zz in range(4):
            self.p.sent(block, self.aside.at[zz], self.spare)
            self.p.went_onward(zz, lambda d: self.p.sent(block, self.along.at[zz, d], self.spare))


def gather_body(
    x_ref, seg_ref, ga_ref, bq_ref, gf_ref, wq_ref, wo_ref, wg_ref, wu_ref, c_ref,
    WQ_out, WO_out, G, C, cos_out, sin_out, gains_out, q_out, k_out, v_out, p_out, att_out, a1_out, mid_out, a2_out,
    WQ, WO, vg, vu, GS, CS, S, bias, cos_ref, sin_ref, gains, queries, keys, values, probs, att, a1, mid, a2,
    rq, ro, rg, rc, rs, szq, syq, sdq, szo, syo, sdo, sg, sdg, scz, scy, ss, loc, written,
):
    p = Place()
    r, s, c, z = p.r, p.s, p.c, p.z
    spare = loc.at[0]
    own = rows_of(192 * s, 192)
    own_c = rows_of(128 * s, 128, 128)
    loads = (
        pltpu.make_async_copy(wq_ref, WQ.at[own], loc.at[1]),
        pltpu.make_async_copy(wo_ref, WO.at[own], loc.at[2]),
        pltpu.make_async_copy(wg_ref, vg, loc.at[3]),
        pltpu.make_async_copy(wu_ref, vu, loc.at[4]),
        pltpu.make_async_copy(c_ref, CS, loc.at[5]),
    )
    for copy in loads:
        copy.start()
    p.greet(range(1, 8))
    gap = jnp.zeros((1, 64), F32)
    small = jnp.concatenate(
        [ga_ref[...].astype(F32)[None], gap, bq_ref[...].astype(F32)[None], gf_ref[...].astype(F32)[None], gap],
        axis=1,
    )
    S[s] = jnp.broadcast_to(small, (16, 768)).astype(BF)

    def vq(t, q):
        return WQ.at[quarter(t, q)]

    def vo(t, q):
        return WO.at[quarter(t, q)]

    def gq(t, q):
        return G.at[quarter(t, q)]

    def cot_block(t):
        return C.at[rows_of(128 * t, 128, 128)]

    g_q = Gather(p, spare, lambda t: vq(t, r), lambda t: rq.at[t, r], szq, syq)
    g_o = Gather(p, spare, lambda t: vo(t, r), lambda t: ro.at[t, r], szo, syo)
    g_c = Gather(p, spare, cot_block, lambda t: rc.at[t], scz, scy)

    def share(view, sems, rsems):
        def to_replicas(t):
            v = view(t, r)
            send(v, v, sems.at[t, 0], rsems.at[t, r], p.across)
            send(v, v, sems.at[t, 1], rsems.at[t, r], p.core)

        return to_replicas

    def relay(view, sems, rsems, t):
        v = view(t, p.rx)
        p.arrived(v, rsems.at[t, p.rx], spare)
        send(v, v, sems.at[t, 2], rsems.at[t, p.rx], p.core)

    def from_core(view, rsems):
        @pl.loop(1, 8)
        def _(k):
            t = (s + k) % 8
            p.arrived(view(t, p.rc), rsems.at[t, p.rc], spare)
            p.arrived(view(t, p.rd), rsems.at[t, p.rd], spare)

    share_q, share_o, share_g = share(vq, sdq, rq), share(vo, sdo, ro), share(gq, sdg, rg)

    def owner(k):
        return 2 * ((z + 1 + k // 2) % 4) + (p.y if k % 2 else 1 - p.y)

    def source(k):
        return 2 * ((z + 3 - k // 2) % 4) + (p.y if k % 2 else 1 - p.y)

    def along(k):
        return p.mine(p.line(k)) if k < 4 else p.theirs(p.line(k - 4))

    def q_step(k):
        g_q.step(k, share_q)

    def q_other(k):
        g_q.other(k, share_q)

    def q_relay(k):
        relay(vq, sdq, rq, along(k))

    def o_start():
        g_o.start(wo_ref.at[rows_of(48 * r, 48)])

    def o_step(k):
        g_o.step(k, share_o)

    def o_other(k):
        g_o.other(k, share_o)

    def o_relay(k):
        relay(vo, sdo, ro, along(k))

    def c_start():
        g_c.start(CS)

    def give(k):
        t = owner(k)
        send(GS.at[t, rows_of(48 * r, 48)], gq(s, r), sg.at[t], rg.at[s, r], p.peer(t))

    def take(k):
        t = source(k)
        p.arrived(gq(t, r), rg.at[t, r], spare)
        share_g(t)

    def g_relay(k):
        relay(gq, sdg, rg, source(k))

    own_out = (
        pltpu.make_async_copy(GS.at[s], G.at[own], loc.at[1]),
        pltpu.make_async_copy(CS, C.at[own_c], loc.at[2]),
    )
    save = (pltpu.make_async_copy(WQ, WQ_out, loc.at[3]), pltpu.make_async_copy(WO, WO_out, loc.at[4]))
    results = tuple(
        pltpu.make_async_copy(ref, out, written.at[i])
        for i, (ref, out) in enumerate(
            (
                (cos_ref, cos_out), (sin_ref, sin_out), (gains, gains_out), (a1, a1_out), (queries, q_out), (keys, k_out),
                (values, v_out), (probs, p_out), (att, att_out), (mid, mid_out), (a2, a2_out),
            )
        )
    )
    kept = {}

    def prepare():
        for copy in loads:
            copy.wait()
        zeros = jnp.zeros((192, 32), BF)
        for t in range(8):
            GS[t, :, 0:1120] = vg[:, 1120 * t : 1120 * t + 1120]
            GS[t, :, 1120:1152] = zeros
            GS[t, :, 1152:2272] = vu[:, 1120 * t : 1120 * t + 1120]
            GS[t, :, 2272:2304] = zeros
        for copy in own_out:
            copy.start()
        across = jnp.broadcast_to(seg_ref[...].astype(F32), (128, 128))
        down = across.T
        row = lax.broadcasted_iota(jnp.int32, (128, 128), 0)
        column = lax.broadcasted_iota(jnp.int32, (128, 128), 1)
        earlier = jnp.sum(jnp.where(across < down, 1.0, 0.0), axis=1, keepdims=True)
        position = row.astype(F32) - earlier
        half = (column - 64 * (column // 64)).astype(F32)
        angle = position * jnp.exp(half * (-2.0 * math.log(rope_base) / HEAD_DIMENSION))
        cos_ref[...] = jnp.cos(angle)
        sin_ref[...] = jnp.where(column < 64, -1.0, 1.0) * jnp.sin(angle)
        kept["open"] = (across == down) & (column <= row)

    def first_norm():
        @pl.loop(1, 8)
        def _(k):
            t = (s + k) % 8
            p.arrived(S.at[t], rs.at[t], spare)

        for t in range(8):
            row = S[t, 0:1, :].astype(F32)
            gains[0:1, 192 * t : 192 * t + 192] = row[:, 0:192]
            bias[0:1, 256 * t : 256 * t + 256] = row[:, 256:512]
            gains[1:2, 192 * t : 192 * t + 192] = row[:, 512:704]
        x = x_ref[...].astype(F32)
        a1[...] = (x * inverse_norm(x) * gains[0:1, :]).astype(BF)

    def q_all():
        from_core(vq, rq)

    def o_all():
        from_core(vo, ro)

    def attend():
        cosine, sine = cos_ref[...], sin_ref[...]
        for j in range(4):
            co = pl.ds(512 * j, 512)
            joined = dot(a1[...], WQ[:, co]) + bias[0:1, co]
            for i in range(4):
                h = 4 * j + i
                u = joined[:, 128 * i : 128 * i + 128]
                if h < 14:
                    u = u * cosine + pltpu.roll(u, 64, 1) * sine
                if h < 12:
                    queries[h // 6, pl.ds(128 * (h % 6), 128), :] = (u * HEAD_DIMENSION**-0.5).astype(BF)
                elif h < 14:
                    keys[h - 12] = u.astype(BF)
                else:
                    values[h - 14] = u.astype(BF)
        save[0].start()
        for g in range(2):
            scores = dot_nt(queries[g], keys[g]).reshape(6, 128, 128)
            scores = jnp.where(kept["open"][None], scores, -1e30)
            ex = jnp.exp(scores - jnp.max(scores, axis=-1, keepdims=True))
            soft = (ex / jnp.sum(ex, axis=-1, keepdims=True)).reshape(768, 128)
            probs[g] = soft.astype(BF)
            out = dot(probs[g], values[g]).astype(BF)
            for i in range(6):
                att[:, pl.ds(128 * (6 * g + i), 128)] = out[128 * i : 128 * i + 128]
        for copy in results[0:9]:
            copy.start()

    def second_norm():
        save[1].start()
        x = x_ref[...].astype(F32)
        for j in range(3):
            co = pl.ds(512 * j, 512)
            mid[:, co] = x[:, 512 * j : 512 * j + 512] + dot(att[...], WO[:, co])
        hidden = mid[...]
        a2[...] = (hidden * inverse_norm(hidden) * gains[1:2, :]).astype(BF)
        for copy in results[9:11]:
            copy.start()

    at_end = (z == 0) | (z == 3)
    in_middle = (z == 1) | (z == 2)
    g_q.start(wq_ref.at[rows_of(48 * r, 48)])
    for k in range(1, 8):
        t = (s + k) % 8
        send(S.at[s], S.at[s], ss.at[t], rs.at[s], p.peer(t))
    prepare()

    @pl.when(at_end)
    def _():
        q_other(0)
        o_start()
        give(0)
        give(1)
        give(6)
        q_step(1)
        o_other(0)
        c_start()
        o_step(1)
        take(0)
        take(6)
        give(5)
        o_step(2)
        q_relay(4)
        q_other(1)
        q_step(3)


    @pl.when(in_middle)
    def _():
        o_start()
        give(1)
        q_step(1)
        give(0)
        give(6)

    q_step(2)
    first_norm()

    @pl.when(at_end)
    def _():
        o_step(3)
        o_relay(1)
        q_relay(3)
        q_other(3)
        q_relay(1)
        take(5)
        o_other(2)
        take(1)
        q_relay(5)
        o_relay(4)
        o_relay(3)
        give(3)
        q_relay(2)
        q_other(2)
        give(4)
        g_c.step(1)
        give(2)
        g_relay(1)
        o_other(3)
        o_other(1)
        o_relay(7)
        take(4)
        take(2)
        q_relay(6)
        g_c.step(2)
        q_relay(7)
        g_c.step(3)
        o_relay(6)
        g_relay(0)


    @pl.when(in_middle)
    def _():
        q_other(0)
        o_step(1)
        o_step(2)
        q_relay(4)
        q_step(3)
        give(5)
        take(1)
        q_other(1)
        o_step(3)
        o_relay(1)
        o_other(0)
        c_start()
        give(2)
        q_relay(1)
        g_relay(1)
        give(4)
        q_other(3)
        take(5)
        o_other(2)
        g_c.step(1)
        give(3)
        q_relay(5)
        take(0)
        take(6)
        q_relay(3)
        q_other(2)
        g_c.step(2)
        o_other(1)
        q_relay(2)
        o_relay(3)
        o_relay(6)
        g_relay(0)
        o_relay(4)
        q_relay(6)
        q_relay(7)
        take(4)
        o_other(3)
        g_c.step(3)
        g_relay(5)
        take(2)

    q_all()
    g_relay(6)
    attend()
    o_relay(5)

    @pl.when(at_end)
    def _():
        o_relay(2)
        g_relay(5)
        take(3)


    @pl.when(in_middle)
    def _():
        o_relay(7)
        take(3)
        o_relay(2)

    g_relay(2)
    o_all()
    g_relay(4)
    g_relay(3)
    second_norm()
    from_core(gq, rg)

    @pl.loop(0, 4)
    def _(k):
        g_c.other(k)

    g_q.finish()
    g_o.finish()
    g_c.finish()

    @pl.loop(1, 8)
    def _(k):
        t = (s + k) % 8
        p.sent(S.at[t], ss.at[t], spare)
        p.sent(gq(t, r), sg.at[t], spare)
        for d in range(3):
            p.sent(vq(t, r), sdq.at[t, d], spare)
            p.sent(vo(t, r), sdo.at[t, d], spare)
            p.sent(gq(t, r), sdg.at[t, d], spare)

    for copy in own_out + save + results:
        copy.wait()


def gather_weights(x, segments, gain_attn, b_qkv, gain_ffn, w_qkv, w_out, w_gate, w_up, cot):
    return pl.pallas_call(
        gather_body,
        out_shape=(
            shaped(1536, 2048), shaped(1536, 1536), shaped(1536, 2304), shaped(1024, 1536), shaped(128, 128, dtype=F32),
            shaped(128, 128, dtype=F32), shaped(8, 1536, dtype=F32), shaped(2, 768, 128), shaped(2, 128, 128), shaped(2, 128, 128), shaped(2, 768, 128),
            shaped(128, 1536), shaped(128, 1536), shaped(128, 1536, dtype=F32), shaped(128, 1536),
        ),
        in_specs=[VMEM] * 5 + [HBM] * 5,
        out_specs=(HBM,) * 15,
        scratch_shapes=[
            low(1536, 2048), low(1536, 1536), low(192, 8960), low(192, 8960), low(8, 192, 2304), low(128, 1536),
            low(8, 16, 768), full(8, 2048), full(128, 128), full(128, 128), full(8, 1536), low(2, 768, 128), low(2, 128, 128),
            low(2, 128, 128), low(2, 768, 128), low(128, 1536), low(128, 1536), full(128, 1536), low(128, 1536),
            DMA((8, 4)), DMA((8, 4)), DMA((8, 4)), DMA((8,)), DMA((8,)),
            DMA((4, 2)), DMA((4,)), DMA((8, 3)), DMA((4, 2)), DMA((4,)), DMA((8, 3)),
            DMA((8,)), DMA((8, 3)), DMA((4, 2)), DMA((4,)), DMA((8,)), DMA((6,)), DMA((11,)),
        ],
        compiler_params=pltpu.CompilerParams(collective_id=0, has_side_effects=True, vmem_limit_bytes=56 << 20),
        name="gather_and_attend",
    )(x, segments, gain_attn, b_qkv, gain_ffn, w_qkv, w_out, w_gate, w_up, cot)


class RowSums:
    def __init__(self, p, spare, total, chip, side, far, across, out, sems, width):
        self.p, self.spare, self.total, self.chip, self.side = p, spare, total, chip, side
        self.far, self.across, self.out, self.sems = far, across, out, sems
        self.width = width

    def part(self, t, q):
        return self.total.at[quarter(t, q), 0 : self.width]

    def slot(self, t, xx):
        return self.chip.at[t, xx, :, 0 : self.width]

    def own(self, k):
        p = self.p
        return 2 * p.line(3 - k % 4) + (1 - p.y + (k // 4) * (2 * p.y - 1))

    def to_core(self, t):
        p = self.p
        for xx in range(2):
            send(
                self.part(t, 2 * xx + 1 - p.c), self.slot(t, xx),
                self.sems[0].at[t, xx], self.sems[1].at[t, xx], p.core,
            )

    def add(self, t, q, ref, sem):
        self.p.arrived(ref, sem, self.spare)
        total = self.part(t, q)
        total[...] = (total[...].astype(F32) + ref[...].astype(F32)).astype(BF)

    def on_chip(self, k):
        p, t = self.p, self.own(k)
        for xx in range(2):
            self.add(t, 2 * xx + p.c, self.slot(t, xx), self.sems[1].at[t, xx])

    def aside(self, k):
        p, t = self.p, self.own(k)
        for xx in range(2):
            at = t // 2, xx
            send(self.part(t, 2 * xx + p.c), self.side.at[at], self.sems[2].at[at], self.sems[3].at[at], p.side)

    def on_line(self, k):
        p = self.p
        zz = p.line(3 - k)
        t = p.mine(zz)
        for xx in range(2):
            q = 2 * xx + p.c
            self.add(t, q, self.side.at[zz, xx], self.sems[3].at[zz, xx])
            p.reduce_step(
                zz,
                lambda slot: self.add(t, q, self.far.at[slot, xx], self.sems[5].at[slot, xx]),
                lambda slot, device: send(
                    self.part(t, q), self.far.at[slot, xx], self.sems[4].at[zz, xx], self.sems[5].at[slot, xx], device
                ),
            )

    def at_owner(self):
        p = self.p
        for xx in range(2):
            send(self.part(p.s, 2 * xx + p.c), self.across.at[xx], self.sems[6].at[xx], self.sems[7].at[xx], p.across)

    def spread(self):
        p = self.p
        for xx in range(2):
            q = 2 * xx + p.c
            p.sent(self.across.at[xx], self.sems[6].at[xx], self.spare)
            self.add(p.s, q, self.across.at[xx], self.sems[7].at[xx])
            total = self.part(p.s, q)
            pltpu.make_async_copy(total, self.out.at[q], self.sems[6].at[4 + xx]).start()
            send(total, self.out.at[q], self.sems[6].at[2 + xx], self.sems[7].at[2 + xx], p.core)

    def finish(self):
        p = self.p
        for xx in range(2):
            q = 2 * xx + 1 - p.c
            p.arrived(self.out.at[q], self.sems[7].at[2 + xx], self.spare)
            p.sent(self.out.at[q], self.sems[6].at[2 + xx], self.spare)
            pltpu.make_async_copy(self.part(p.s, 0), self.out.at[q], self.sems[6].at[4 + xx]).wait()

        @pl.loop(0, 8)
        def _(t):
            for xx in range(2):
                p.sent(self.slot(t, xx), self.sems[0].at[t, xx], self.spare)

        @pl.loop(0, 4)
        def _(i):
            for xx in range(2):
                p.sent(self.side.at[i, xx], self.sems[2].at[i, xx], self.spare)

                @pl.when(i != p.z)
                def _():
                    p.sent(self.far.at[i, xx], self.sems[4].at[i, xx], self.spare)

    @staticmethod
    def buffers(width):
        return [low(8, 2, 48, width), low(4, 2, 48, width), low(5, 2, 48, width), low(2, 48, width)]

    @staticmethod
    def semaphores():
        return [DMA((8, 2)), DMA((8, 2)), DMA((4, 2)), DMA((4, 2)), DMA((4, 2)), DMA((5, 2)), DMA((6,)), DMA((4,))]


def layer_back_body(
    n_ref, c_hbm, g_hbm, d_hbm, wq_hbm, wo_hbm, att_hbm, a1_hbm, x_hbm, cot_hbm, q_hbm,
    mid_hbm, gains_hbm, cos_hbm, sin_hbm, k_hbm, v_hbm, p_hbm,
    out_ref, gtok_ref, OG, OD, OWq, OWo,
    NC, H, vG, vD, MX, PD, PO, YD, ZD, YO, ZO, YB, ZB, RCd, RXd, RC, RX, dj, AT, SM, mid_ref, gains, cos_ref, sin_ref, keys, values, probs,
    Yq, Zq, RXq, RCo, Yo, Zo, RXo,
    free, rn, syn, szn, ryd, rzd, syd, szd, syo, ryo, szo, rzo, syb, ryb, szb, rzb,
    scd, rcd, sxd, rxd, sfd, rfd, scg, rcg, sx, rx, sa, ra, sf, *sems,
):
    p = Place()
    r, s, c, y, z = p.r, p.s, p.c, p.y, p.z
    loc = sems[-1]
    spare = loc.at[0]
    q_sums = RowSums(p, spare, H, RC, Yq, Zq, RXq, OWq, sems[0:8], 2176)
    o_sums = RowSums(p, spare, NC, RCo, Yo, Zo, RXo, OWo, sems[8:16], 1536)

    def block(t):
        return NC.at[rows_of(128 * t, 128, 128)]

    def cot_rows(start, size):
        return rows_of(1024 + start, size, 128)

    loads = (
        pltpu.make_async_copy(n_ref, block(s), loc.at[1]),
        pltpu.make_async_copy(c_hbm, NC.at[1024:2048], loc.at[2]),
        pltpu.make_async_copy(g_hbm, vG, loc.at[3]),
        pltpu.make_async_copy(d_hbm, vD.at[0:1120], loc.at[4]),
    )
    for copy in loads:
        copy.start()
    p.greet(range(1, 8))
    g_n = Gather(p, spare, block, lambda t: rn.at[t], szn, syn)
    g_n.start(n_ref)
    vD[1120:1152, :] = jnp.zeros((32, 1536), BF)
    for copy in loads:
        copy.wait()

    def side(P, Y, ssem, rsem, k):
        zz = p.line(k)
        send(P.at[p.theirs(zz)], Y.at[zz], ssem.at[zz], rsem.at[zz], p.side)

    def side_d(k):
        side(PD, YD, syd, ryd, k)

    def line_step(P, Y, Z, ry, sz, rz, k):
        zz = p.line(k)
        t = p.mine(zz)

        def add(ref, sem):
            p.arrived(ref, sem, spare)
            P[t] = (P[t].astype(F32) + ref[...].astype(F32)).astype(BF)

        add(Y.at[zz], ry.at[zz])
        p.reduce_step(
            zz,
            lambda slot: add(Z.at[slot], rz.at[slot]),
            lambda slot, device: send(P.at[t], Z.at[slot], sz.at[zz], rz.at[slot], device),
        )

    def step_d(k):
        line_step(PD, YD, ZD, ryd, szd, rzd, k)

    def side_oa(k):
        zz = p.line(k)
        send(PO.at[p.theirs(zz), :, 0:768], YO.at[zz], syo.at[zz], ryo.at[zz], p.side)

    def step_oa(k):
        zz = p.line(k)
        half = PO.at[p.mine(zz), :, 0:768]

        def add(ref, sem):
            p.arrived(ref, sem, spare)
            half[...] = (half[...].astype(F32) + ref[...].astype(F32)).astype(BF)

        add(YO.at[zz], ryo.at[zz])
        p.reduce_step(
            zz,
            lambda slot: add(ZO.at[slot], rzo.at[slot]),
            lambda slot, device: send(half, ZO.at[slot], szo.at[zz], rzo.at[slot], device),
        )

    def step_ob(k):
        zz = p.line(k)
        both = PO.at[pl.ds(2 * zz, 2), :, 768:1536]

        def add(slot):
            p.arrived(ZB.at[slot], rzb.at[slot], spare)
            both[...] = (both[...].astype(F32) + ZB[slot].astype(F32)).astype(BF)

        p.reduce_step(
            zz, add, lambda slot, device: send(both, ZB.at[slot], szb.at[zz], rzb.at[slot], device)
        )

    def side_ob():
        send(PO.at[p.theirs(z), :, 768:1536], YB, syb, ryb, p.side)

    at_end = (z == 0) | (z == 3)
    in_middle = (z == 1) | (z == 2)
    g_n.step(1)

    @pl.loop(0, 4)
    def _(k):
        zz = p.line(k)
        pl.when(at_end & (k > 0) & (k < 3))(lambda: g_n.step(k + 1))
        pl.when(in_middle & (k < 2))(lambda: g_n.step(k + 2))
        g_n.other(k)
        rows = rows_of(256 * zz, 256, 256)
        X = NC[rows]
        cot = NC[cot_rows(256 * zz, 256)]
        for j in range(3):
            ga, ua = pl.ds(384 * j, 384), pl.ds(1152 + 384 * j, 384)
            gate = dot(X, vG[:, ga])
            up = dot(X, vG[:, ua])
            d_mixed = dot_nt(cot, vD[ga])
            sg = jax.nn.sigmoid(gate)
            active = gate * sg
            d_active = d_mixed * up
            MX[rows, ga] = (active * up).astype(BF)
            H[rows, ga] = (d_active * sg + d_active * active * (1.0 - sg)).astype(BF)
            H[rows, ua] = (d_mixed * active).astype(BF)
        for j in range(3):
            co = pl.ds(512 * j, 512)
            part = dot_nt(H[rows], vG[co]).astype(BF)
            PD[2 * zz, :, co] = part[:128]
            PD[2 * zz + 1, :, co] = part[128:]
        pl.when(k == 2)(lambda: side_d(1))
        pl.when(k == 3)(lambda: side_d(3))
        for j in range(3):
            co = pl.ds(512 * j, 512)
            part = dot(MX[rows], vD[:, co]).astype(BF)
            PO[2 * zz, :, co] = part[:128]
            PO[2 * zz + 1, :, co] = part[128:]
        pl.when(at_end & (k == 1))(lambda: step_ob(1))
        pl.when(at_end & (k == 2))(lambda: step_ob(2))

    side_d(2)
    side_d(0)

    def owner(k):
        return 2 * ((z + 1 + k // 2) % 4) + (k % 2) * (2 * y - 1) + 1 - y

    def pair_chip(k):
        t = owner(k)
        for xx in range(2):
            p.arrived(RC.at[t, xx], rcg.at[t, xx], spare)
            q = quarter(t, 2 * xx + c)
            vG[q] = (vG[q].astype(F32) + RC[t, xx].astype(F32)).astype(BF)
        send(vG.at[quarter(t, p.rx)], RX.at[t], sx.at[t], rx.at[t], p.across)

    @pl.loop(0, 5)
    def _(j):
        @pl.when(j < 4)
        def _():
            pair = (z + 1 + j) % 4
            rows = rows_of(384 * pair, 384, 128)
            X = NC[0:1024, rows].T
            for i in range(3):
                co = pl.ds(768 * i, 768)
                vG[rows, co] = dot(X, H[0:1024, co]).astype(BF)
            for i in range(2):
                t = owner(2 * j + i)
                for xx in range(2):
                    send(vG.at[quarter(t, 2 * xx + 1 - c)], RC.at[t, xx], scg.at[t, xx], rcg.at[t, xx], p.core)

        @pl.when(j > 0)
        def _():
            pair_chip(2 * j - 2)
            pair_chip(2 * j - 1)

    pl.semaphore_signal(free, inc=1, device_id=p.core, device_id_type=MESH)

    def chunk(i):
        return rows_of(384 * i, 384, 128)

    def cols(q):
        return rows_of(384 * q, 384, 128)

    held = (
        pltpu.make_async_copy(wo_hbm, NC.at[0:1536], loc.at[1]),
        pltpu.make_async_copy(wq_hbm, H.at[:, 0:2048], loc.at[2]),
        pltpu.make_async_copy(att_hbm, NC.at[1536:1664], loc.at[3]),
        pltpu.make_async_copy(a1_hbm, NC.at[1664:1792], loc.at[4]),
        pltpu.make_async_copy(x_hbm, NC.at[1792:1920], loc.at[5]),
        pltpu.make_async_copy(cot_hbm, NC.at[1920:2048], loc.at[6]),
        pltpu.make_async_copy(q_hbm.at[0], MX.at[0:768, 256:384], loc.at[8]),
        pltpu.make_async_copy(q_hbm.at[1], MX.at[0:768, 384:512], loc.at[9]),
        pltpu.make_async_copy(mid_hbm, mid_ref, loc.at[10]),
        pltpu.make_async_copy(gains_hbm, gains, loc.at[11]),
        pltpu.make_async_copy(cos_hbm, cos_ref, loc.at[12]),
        pltpu.make_async_copy(sin_hbm, sin_ref, loc.at[13]),
        pltpu.make_async_copy(k_hbm, keys, loc.at[14]),
        pltpu.make_async_copy(v_hbm, values, loc.at[15]),
        pltpu.make_async_copy(p_hbm, probs, loc.at[16]),
    )

    def down_terms():
        @pl.loop(0, 3)
        def _(i):
            X = MX[:, chunk(i)].T
            for j in range(3):
                co = pl.ds(512 * j, 512)
                vD[chunk(i), co] = dot(X, NC[1024:2048, co]).astype(BF)
            for xx in range(2):
                q = 2 * xx + 1 - c
                send(vD.at[chunk(i), cols(q)], RCd.at[xx, chunk(i)], scd.at[i, xx], rcd.at[i, xx], p.core)

        g_n.finish()
        for copy in held:
            copy.start()

        @pl.loop(0, 3)
        def _(i):
            for xx in range(2):
                p.arrived(RCd.at[xx, chunk(i)], rcd.at[i, xx], spare)
                q = cols(2 * xx + c)
                vD[chunk(i), q] = (vD[chunk(i), q].astype(F32) + RCd[xx, chunk(i)].astype(F32)).astype(BF)

    def pair_whole(k):
        t = owner(k)
        q = quarter(t, r)
        p.arrived(RX.at[t], rx.at[t], spare)
        vG[q] = (vG[q].astype(F32) + RX[t].astype(F32)).astype(BF)

        if k < 7:
            send(vG.at[q], OG.at[r, s], sa.at[t], ra.at[s, r], p.peer(t))
        else:
            pltpu.make_async_copy(vG.at[q], OG.at[r, s], loc.at[7]).start()

    def share(t):
        v = OG.at[r, t]
        send(v, v, sf.at[t, 0], ra.at[t, r], p.across)
        send(v, v, sf.at[t, 1], ra.at[t, r], p.core)

    def source(k):
        return 2 * ((z + 3 - k // 2) % 4) + (1 - y if k % 2 == 0 else y)

    def take(k):
        t = source(k)
        if k < 7:
            p.arrived(OG.at[r, t], ra.at[t, r], spare)
        else:
            pltpu.make_async_copy(vG.at[quarter(s, r)], OG.at[r, s], loc.at[7]).wait()
        share(t)

    def relay(k):
        t = source(k)
        v = OG.at[p.rx, t]
        p.arrived(v, ra.at[t, p.rx], spare)
        send(v, v, sf.at[t, 2], ra.at[t, p.rx], p.core)

    def down_across(i):
        send(vD.at[chunk(i), cols(p.rx)], RXd.at[chunk(i)], sxd.at[i], rxd.at[i], p.across)

    def down_whole(i):
        p.arrived(RXd.at[chunk(i)], rxd.at[i], spare)
        q = cols(r)
        vD[chunk(i), q] = (vD[chunk(i), q].astype(F32) + RXd[chunk(i)].astype(F32)).astype(BF)
        src, dst = vD.at[chunk(i), q], OD.at[r, chunk(i)]
        pltpu.make_async_copy(src, dst, sfd.at[i, 3]).start()
        send(src, dst, sfd.at[i, 0], rfd.at[i, r], p.across)
        send(src, dst, sfd.at[i, 1], rfd.at[i, r], p.core)

    def down_relay(i):
        v = OD.at[p.rx, chunk(i)]
        p.arrived(v, rfd.at[i, p.rx], spare)
        send(v, v, sfd.at[i, 2], rfd.at[i, p.rx], p.core)

    def back(w):
        return w * cos_ref[...] - pltpu.roll(w, 64, 1) * sin_ref[...]

    kept = {}

    def attention_out():
        for copy in held:
            copy.wait()
        dn, hidden = PD[s].astype(F32), mid_ref[...]
        rstd = inverse_norm(hidden)
        unit = hidden * rstd
        kept["ffn"] = jnp.sum(dn * unit, axis=0, keepdims=True)
        e = dn * gains[1:2, :]
        dm = NC[1920:2048].astype(F32) + rstd * (e - unit * jnp.mean(e * unit, axis=-1, keepdims=True))
        NC[1920:2048] = dm.astype(BF)
        AT[...] = NC[1536:1664].T
        for j in range(3):
            part = dot_nt(NC[1920:2048], NC[pl.ds(512 * j, 512)]).astype(BF)
            for i in range(4):
                h = 4 * j + i
                MX[pl.ds(128 * (h % 6), 128), pl.ds(128 * (h // 6), 128)] = part[:, 128 * i : 128 * i + 128]
        for j in range(3):
            co = pl.ds(512 * j, 512)
            NC[0:1536, co] = dot(AT[...], NC[1920:2048, co]).astype(BF)

        @pl.loop(0, 8)
        def _(k):
            o_sums.to_core(o_sums.own(k))

    def heads(g):
        grad = MX[0:768, 128 * g : 128 * g + 128]
        query = MX[0:768, 256 + 128 * g : 384 + 128 * g]
        soft = probs[g].astype(F32)
        d_probs = dot_nt(grad, values[g])
        d_scores = (soft * (d_probs - jnp.sum(soft * d_probs, axis=-1, keepdims=True))).astype(BF)
        d_values = dot(probs[g].T, grad)
        d_queries = dot(d_scores, keys[g]) * HEAD_DIMENSION**-0.5
        d_keys = dot(d_scores.T, query)
        for i in range(6):
            dj[:, pl.ds(128 * (6 * g + i), 128)] = back(d_queries[128 * i : 128 * i + 128]).astype(BF)
        dj[:, pl.ds(128 * (12 + g), 128)] = back(d_keys).astype(BF)
        dj[:, pl.ds(128 * (14 + g), 128)] = d_values.astype(BF)

    def attention_in():
        heads(1)
        joined_grad = dj[...]
        bias_grad = jnp.sum(joined_grad.astype(F32), axis=0, keepdims=True)
        x = NC[1792:1920].astype(F32)
        rstd = inverse_norm(x)
        unit = x * rstd
        dn1 = jnp.concatenate(
            [dot_nt(joined_grad, H[pl.ds(512 * j, 512), 0:2048]) for j in range(3)], axis=1
        )
        gain_attn_grad = jnp.sum(dn1 * unit, axis=0, keepdims=True)
        e = dn1 * gains[0:1, :]
        NC[1792:1920] = (
            NC[1920:2048].astype(F32) + rstd * (e - unit * jnp.mean(e * unit, axis=-1, keepdims=True))
        ).astype(BF)
        pltpu.make_async_copy(NC.at[1792:1920], gtok_ref, loc.at[5]).start()
        SM[...] = jnp.zeros_like(SM)
        ffn = kept["ffn"]
        for t in range(8):
            SM[t, 0:1, :] = gain_attn_grad[:, 192 * t : 192 * t + 128]
            SM[t, 1:2, 0:64] = gain_attn_grad[:, 192 * t + 128 : 192 * t + 192]
            SM[t, 2:3, :] = bias_grad[:, 256 * t : 256 * t + 128]
            SM[t, 3:4, :] = bias_grad[:, 256 * t + 128 : 256 * t + 256]
            SM[t, 4:5, :] = ffn[:, 192 * t : 192 * t + 128]
            SM[t, 5:6, 0:64] = ffn[:, 192 * t + 128 : 192 * t + 192]
        AT[...] = NC[1664:1792].T

    def joined_terms():
        pl.semaphore_wait(free, 1)

        @pl.loop(0, 8)
        def _(k):
            t = q_sums.own(k)
            rows = rows_of(192 * t, 192)
            for j in range(2):
                co = pl.ds(1024 * j, 1024)
                H[rows, co] = dot(AT[rows], dj[:, co]).astype(BF)
            H[rows, 2048:2176] = jnp.zeros((192, 128), BF)
            H[rows_of(192 * t, 16), 2048:2176] = SM[t].astype(BF)
            q_sums.to_core(t)

    def on_chip(sums):
        @pl.loop(0, 8)
        def _(k):
            sums.on_chip(k)

    def finish_out():
        p.arrived(YB, ryb, spare)
        PO[s, :, 768:1536] = (PO[s, :, 768:1536].astype(F32) + YB[...].astype(F32)).astype(BF)
        PO[s] = (PO[s].astype(F32) + mid_ref[...]).astype(BF)
        pltpu.make_async_copy(PO.at[s], out_ref, loc.at[6]).start()

    def first_heads():
        heads(0)

    def o_on_chip():
        on_chip(o_sums)

    def q_on_chip():
        on_chip(q_sums)


    @pl.when(at_end)
    def _():
        step_d(3)
        side_oa(3)
        step_d(2)
        side_oa(2)
        side_oa(0)
        step_d(1)
        pair_whole(3)


    @pl.when(in_middle)
    def _():
        side_oa(2)
        side_oa(0)
        step_ob(2)
        step_d(3)
        step_d(2)
        step_d(1)
        pair_whole(6)

    down_terms()

    @pl.when(at_end)
    def _():
        step_ob(3)
        pair_whole(6)
        down_across(1)
        pair_whole(5)
        step_oa(3)
        pair_whole(0)
        down_across(0)
        side_oa(1)


    @pl.when(in_middle)
    def _():
        side_oa(3)
        pair_whole(5)
        down_across(0)
        side_oa(1)
        pair_whole(3)
        take(3)
        pair_whole(1)
        down_across(1)
        pair_whole(2)

    step_d(0)
    attention_out()

    @pl.when(at_end)
    def _():
        down_across(2)

    first_heads()
    attention_in()

    @pl.when(at_end)
    def _():
        pair_whole(4)
        pair_whole(2)

    joined_terms()

    @pl.when(in_middle)
    def _():
        pair_whole(4)

    o_on_chip()

    @pl.when(at_end)
    def _():
        o_sums.aside(2)
        take(3)
        o_sums.aside(0)
        pair_whole(1)
        take(6)


    @pl.when(in_middle)
    def _():
        down_across(2)
        o_sums.aside(2)
        pair_whole(7)
        down_whole(0)
        o_sums.aside(0)
        step_oa(3)
        pair_whole(0)
        take(7)

    q_on_chip()

    @pl.when(at_end)
    def _():
        q_sums.aside(0)
        take(2)
        q_sums.aside(1)
        down_whole(1)
        take(5)
        down_whole(0)
        pair_whole(7)
        o_sums.on_line(0)
        down_whole(2)
        take(1)
        q_sums.aside(2)
        take(7)
        q_sums.on_line(0)
        o_sums.aside(1)
        take(4)
        relay(5)
        q_sums.aside(3)
        q_sums.on_line(1)
        q_sums.on_line(2)
        step_ob(0)
        take(0)
        o_sums.on_line(1)
        o_sums.aside(3)
        q_sums.on_line(3)
        q_sums.at_owner()
        o_sums.on_line(2)
        relay(2)
        relay(3)
        step_oa(2)
        relay(4)
        o_sums.on_line(3)
        o_sums.at_owner()
        q_sums.spread()
        step_oa(1)
        down_relay(2)
        down_relay(0)
        relay(1)
        relay(6)
        relay(7)
        relay(0)
        side_ob()
        down_relay(1)
        step_oa(0)
        finish_out()
        o_sums.spread()


    @pl.when(in_middle)
    def _():
        q_sums.aside(1)
        q_sums.aside(0)
        take(4)
        take(6)
        down_whole(1)
        take(5)
        relay(3)
        step_ob(3)
        take(2)
        take(1)
        q_sums.aside(2)
        o_sums.on_line(0)
        q_sums.aside(3)
        o_sums.aside(1)
        down_whole(2)
        step_ob(1)
        q_sums.on_line(0)
        relay(5)
        o_sums.aside(3)
        q_sums.on_line(1)
        q_sums.on_line(2)
        step_ob(0)
        take(0)
        q_sums.on_line(3)
        q_sums.at_owner()
        relay(4)
        o_sums.on_line(2)
        side_ob()
        relay(2)
        o_sums.on_line(1)
        relay(6)
        o_sums.on_line(3)
        o_sums.at_owner()
        relay(0)
        step_oa(1)
        down_relay(1)
        down_relay(2)
        relay(7)
        down_relay(0)
        q_sums.spread()
        relay(1)
        step_oa(2)
        o_sums.spread()
        step_oa(0)
        finish_out()

    o_sums.finish()
    q_sums.finish()
    pltpu.make_async_copy(NC.at[1792:1920], gtok_ref, loc.at[5]).wait()
    pltpu.make_async_copy(PO.at[s], out_ref, loc.at[6]).wait()

    @pl.loop(0, 3)
    def _(i):
        for q in (p.rc, p.rd):
            p.arrived(OD.at[q, chunk(i)], rfd.at[i, q], spare)
        for d in range(3):
            p.sent(OD.at[r, chunk(i)], sfd.at[i, d], spare)
        pltpu.make_async_copy(OD.at[r, chunk(i)], OD.at[r, chunk(i)], sfd.at[i, 3]).wait()
        for xx in range(2):
            p.sent(RCd.at[xx, chunk(i)], scd.at[i, xx], spare)
        p.sent(RXd.at[chunk(i)], sxd.at[i], spare)

    @pl.loop(0, 8)
    def _(t):
        for q in (p.rc, p.rd):
            p.arrived(OG.at[q, t], ra.at[t, q], spare)
        for d in range(3):
            p.sent(OG.at[r, t], sf.at[t, d], spare)
        for xx in range(2):
            p.sent(RC.at[t, xx], scg.at[t, xx], spare)
        p.sent(RX.at[t], sx.at[t], spare)

        @pl.when(t != s)
        def _():
            p.sent(OG.at[r, s], sa.at[t], spare)

    @pl.loop(0, 4)
    def _(i):
        p.sent(YD.at[i], syd.at[i], spare)
        p.sent(YO.at[i], syo.at[i], spare)

        @pl.when(i != z)
        def _():
            p.sent(ZD.at[i], szd.at[i], spare)
            p.sent(ZO.at[i], szo.at[i], spare)
            p.sent(ZB.at[i], szb.at[i], spare)

    p.sent(YB, syb, spare)


def layer_back(*args):
    return pl.pallas_call(
        layer_back_body,
        out_shape=(
            shaped(128, 1536), shaped(128, 1536), shaped(4, 8, 48, 2304), shaped(4, 1152, 384), shaped(4, 48, 2176),
            shaped(4, 48, 1536),
        ),
        in_specs=[HBM] * 18,
        out_specs=(HBM,) * 6,
        scratch_shapes=[
            low(2048, 1536), low(1536, 2304), low(1536, 2304), low(1152, 1536), low(1024, 1152),
            low(8, 128, 1536), low(8, 128, 1536), low(4, 128, 1536), low(5, 128, 1536), low(4, 128, 768), low(5, 128, 768),
            low(128, 768), low(5, 2, 128, 768),
            low(2, 1152, 384), low(1152, 384), low(8, 2, 48, 2304), low(8, 48, 2304),
            low(128, 2048), low(1536, 128), full(8, 16, 128), full(128, 1536), full(8, 1536), full(128, 128), full(128, 128),
            low(2, 128, 128), low(2, 128, 128), low(2, 768, 128),
            *RowSums.buffers(2176)[1:], *RowSums.buffers(1536),
            pltpu.SemaphoreType.REGULAR, DMA((8,)), DMA((4,)), DMA((4, 2)),
            DMA((4,)), DMA((5,)), DMA((4,)), DMA((4,)), DMA((4,)), DMA((4,)), DMA((4,)), DMA((5,)), DMA, DMA, DMA((4,)), DMA((5,)),
            DMA((3, 2)), DMA((3, 2)), DMA((3,)), DMA((3,)), DMA((3, 4)), DMA((3, 4)),
            DMA((8, 2)), DMA((8, 2)), DMA((8,)), DMA((8,)), DMA((8,)), DMA((8, 4)), DMA((8, 3)),
            *RowSums.semaphores(), *RowSums.semaphores(), DMA((17,)),
        ],
        compiler_params=pltpu.CompilerParams(collective_id=1, has_side_effects=True, vmem_limit_bytes=64 << 20),
        name="layer_back",
    )(*args)


def widen_body(
    g_ref, d_ref, q_ref, o_ref, x_ref, y_ref, gate, up, down, qkv, out, x_out, y_out, ga, bq, gf, narrow
):
    for first, wide in ((0, gate), (1152, up)):
        for t in range(8):
            narrow[:, 1120 * t : 1120 * t + 1120] = g_ref[0, t, :, first : first + 1120]
        wide[...] = narrow[...].astype(F32)
    down[...] = d_ref[0, 0:1120, :].astype(F32)
    qkv[...] = q_ref[0, :, 0:2048].astype(F32)
    out[...] = o_ref[0].astype(F32)
    x_out[...] = x_ref[...]
    y_out[...] = y_ref[...]

    @pl.when(pl.program_id(0) == 0)
    def _():
        small = q_ref[0, 0:16, 2048:2176].astype(F32)
        ga[...] = jnp.concatenate([small[0:1], small[1:2, 0:64]], axis=1)[0]
        bq[...] = jnp.concatenate([small[2:3], small[3:4]], axis=1)[0]
        gf[...] = jnp.concatenate([small[4:5], small[5:6, 0:64]], axis=1)[0]


def widen(g, d, q, o, x, y):
    def rows(size, width):
        return pl.BlockSpec((size, width), lambda i: (i, 0))

    def whole(size):
        return pl.BlockSpec((size,), lambda i: (0,))

    return pl.pallas_call(
        widen_body,
        grid=(4,),
        out_shape=(
            shaped(192, 8960, dtype=F32), shaped(192, 8960, dtype=F32), shaped(1120, 1536, dtype=F32),
            shaped(192, 2048, dtype=F32), shaped(192, 1536, dtype=F32), shaped(128, 1536), shaped(128, 1536),
            shaped(192, dtype=F32), shaped(256, dtype=F32), shaped(192, dtype=F32),
        ),
        in_specs=[
            pl.BlockSpec((1, 8, 48, 2304), lambda i: (i, 0, 0, 0)),
            pl.BlockSpec((1, 1152, 384), lambda i: (i, 0, 0)),
            pl.BlockSpec((1, 48, 2176), lambda i: (i, 0, 0)),
            pl.BlockSpec((1, 48, 1536), lambda i: (i, 0, 0)),
            rows(32, 1536),
            rows(32, 1536),
        ],
        out_specs=(
            rows(48, 8960), rows(48, 8960), pl.BlockSpec((1120, 384), lambda i: (0, i)), rows(48, 2048), rows(48, 1536),
            rows(32, 1536), rows(32, 1536), whole(192), whole(256), whole(192),
        ),
        scratch_shapes=[low(48, 8960)],
        compiler_params=pltpu.CompilerParams(vmem_limit_bytes=62 << 20),
        name="widen",
    )(g, d, q, o, x, y)


def shards_eight(
    tokens, segments, gain_attn, w_qkv, b_qkv, w_out, gain_ffn, w_gate, w_up, w_down, cotangent
):
    x, cot = tokens[0], cotangent[0]
    WQ, WO, G, C, cosine, sine, gains, queries, keys, values, probs, att, a1, mid, a2 = gather_weights(
        x, segments, gain_attn, b_qkv, gain_ffn, w_qkv, w_out, w_gate, w_up, cot
    )
    out, grad_tokens, gate_up, down, qkv, o = layer_back(
        a2, C, G, w_down, WQ, WO, att, a1, x, cot, queries, mid, gains, cosine, sine, keys, values, probs
    )
    gate, up, down, qkv_rows, out_rows, out, grad_tokens, ga, bq, gf = widen(gate_up, down, qkv, o, out, grad_tokens)
    return out[None], grad_tokens[None], ga, qkv_rows, bq, out_rows, gf, gate, up, down


def solution(mesh):
    placed = (
        P(("replica", "shard"), None, None),
        P(("replica", "shard"), None),
        P("shard"),
        P("shard", None),
        P("shard"),
        P("shard", None),
        P("shard"),
        P("shard", None),
        P("shard", None),
        P("shard", None),
        P(("replica", "shard"), None, None),
    )
    return jax.shard_map(
        shards_eight if (mesh.shape["replica"], mesh.shape["shard"]) == (4, 8) else shards,
        mesh=mesh,
        in_specs=placed,
        out_specs=(
            P(("replica", "shard"), None, None),
            P(("replica", "shard"), None, None),
            P("shard"),
            P("shard", None),
            P("shard"),
            P("shard", None),
            P("shard"),
            P("shard", None),
            P("shard", None),
            P("shard", None),
        ),
        check_vma=False,
    )
```

profile of v0, /device:TPU:0, one launch (start us, length us, event | category | flops | bytes accessed | tf_op | source)
XLA Modules:
  0.0 313.5 jit_solution(15792136664531232595)
XLA Ops:
  0.6 104.2 %gather_and_attend.1 = (bf16[1536,2048]{1,0:T(8,128)(2,1)}, bf16[1536,1536]{1,0:T(8,128)(2,1)}, bf16[1536,2304]{1,0:T(8,128)(2,1)}, bf16[1024,1536]{1,0:T(8,128)...) custom-call(bf16[128,1536]{1,0:T(8,128)(2,1)} %bitcast.4, ...), custom_call_target="tpu_custom_call" | custom-call | tf_op jit(solution)/shard_map/gather_and_attend/pallas_call | solution.py:784
  104.9 195.0 %layer_back.1 = (bf16[128,1536]{1,0:T(8,128)(2,1)}, bf16[128,1536]{1,0:T(8,128)(2,1)}, bf16[4,8,48,2304]{3,2,1,0:T(8,128)(2,1)}, bf16[4,1152,384]{2,1,0:T(8,128)...) custom-call(bf16[128,1536]{1,0:T(8,128)(2,1)} %get-tuple-element.41.n_ref, ...), custom_call_target="tpu_custom_call" | custom-call | tf_op jit(solution)/shard_map/layer_back/pallas_call | solution.py:1513
  299.8 13.5 %widen.1 = (f32[192,8960]{1,0:T(8,128)}, f32[192,8960]{1,0:T(8,128)}, f32[1120,1536]{1,0:T(8,128)}, f32[192,2048]{1,0:T(8,128)}, f32[192,1536]{1,0:T(8,128)}, /*...) custom-call(bf16[4,8,48,2304]{3,2,1,0:T(8,128)(2,1)} %get-tuple-element.56.g_r, ...), custom_call_target="tpu_custom_call" | custom-call | tf_op jit(solution)/shard_map/widen/pallas_call | solution.py:1568
where the time goes:
time: 319 us; the launch traced here: 313 us
  Pallas kernels  313 us (98%)
    pallas_call x1, Pallas kernels, layer_back(): pl.pallas_call(layer_back_body, out_shape=(shaped(128, 1536), shaped(128,...  195 us
    pallas_call x1, Pallas kernels, gather_weights(): pl.pallas_call(gather_body, out_shape=(shaped(1536, 2048), shaped(1536, 1...  104 us
    pallas_call x1, Pallas kernels, widen(): pl.pallas_call(widen_body, grid=(4,), out_shape=(shaped(192, 8960, dtype=...  13.5 us

commit v1 on v0

--- a/solution.py
+++ b/solution.py
@@ -1055,6 +1055,8 @@
 
     @pl.loop(0, 5)
     def _(j):
+        pl.when(at_end & (j == 2))(lambda: step_d(3))
+
         @pl.when(j < 4)
         def _():
             pair = (z + 1 + j) % 4
@@ -1275,11 +1277,10 @@
     def q_on_chip():
         on_chip(q_sums)
 
+    side_oa(3)
 
     @pl.when(at_end)
     def _():
-        step_d(3)
-        side_oa(3)
         step_d(2)
         side_oa(2)
         side_oa(0)
@@ -1298,13 +1299,13 @@
         pair_whole(6)
 
     down_terms()
+    pair_whole(5)
 
     @pl.when(at_end)
     def _():
         step_ob(3)
         pair_whole(6)
         down_across(1)
-        pair_whole(5)
         step_oa(3)
         pair_whole(0)
         down_across(0)
@@ -1313,16 +1314,12 @@
 
     @pl.when(in_middle)
     def _():
-        side_oa(3)
-        pair_whole(5)
         down_across(0)
         side_oa(1)
         pair_whole(3)
-        take(3)
-        pair_whole(1)
         down_across(1)
-        pair_whole(2)
-
+
+    pair_whole(2)
     step_d(0)
     attention_out()
 
@@ -1331,27 +1328,27 @@
         down_across(2)
 
     first_heads()
+
+    @pl.when(in_middle)
+    def _():
+        pair_whole(1)
+        take(3)
+
     attention_in()
 
+    @pl.when(in_middle)
+    def _():
+        pair_whole(4)
+
+    joined_terms()
+    o_on_chip()
+
     @pl.when(at_end)
     def _():
-        pair_whole(4)
-        pair_whole(2)
-
-    joined_terms()
-
-    @pl.when(in_middle)
-    def _():
-        pair_whole(4)
-
-    o_on_chip()
-
-    @pl.when(at_end)
-    def _():
-        o_sums.aside(2)
-        take(3)
         o_sums.aside(0)
         pair_whole(1)
+        take(3)
+        pair_whole(4)
         take(6)
 
 
@@ -1370,12 +1367,12 @@
 
     @pl.when(at_end)
     def _():
+        o_sums.aside(2)
         q_sums.aside(0)
         take(2)
         q_sums.aside(1)
         down_whole(1)
         take(5)
-        down_whole(0)
         pair_whole(7)
         o_sums.on_line(0)
         down_whole(2)
@@ -1385,11 +1382,11 @@
         q_sums.on_line(0)
         o_sums.aside(1)
         take(4)
+        q_sums.on_line(1)
         relay(5)
         q_sums.aside(3)
-        q_sums.on_line(1)
+        down_whole(0)
         q_sums.on_line(2)
-        step_ob(0)
         take(0)
         o_sums.on_line(1)
         o_sums.aside(3)
@@ -1402,6 +1399,7 @@
         relay(4)
         o_sums.on_line(3)
         o_sums.at_owner()
+        step_ob(0)
         q_sums.spread()
         step_oa(1)
         down_relay(2)
@@ -1445,18 +1443,18 @@
         q_sums.on_line(3)
         q_sums.at_owner()
         relay(4)
+        relay(2)
         o_sums.on_line(2)
         side_ob()
-        relay(2)
         o_sums.on_line(1)
         relay(6)
+        relay(7)
         o_sums.on_line(3)
         o_sums.at_owner()
         relay(0)
         step_oa(1)
         down_relay(1)
         down_relay(2)
-        relay(7)
         down_relay(0)
         q_sums.spread()
         relay(1)

time: 319 us -> 317 us (level)
  no operation moved by 1% of the time
where the time goes in v1:
time: 317 us; the launch traced here: 314 us
  Pallas kernels  313 us (99%)
    pallas_call x1, Pallas kernels, layer_back(): pl.pallas_call(layer_back_body, out_shape=(shaped(128, 1536), shaped(128,...  195 us
    pallas_call x1, Pallas kernels, gather_weights(): pl.pallas_call(gather_body, out_shape=(shaped(1536, 2048), shaped(1536, 1...  104 us
    pallas_call x1, Pallas kernels, widen(): pl.pallas_call(widen_body, grid=(4,), out_shape=(shaped(192, 8960, dtype=...  13.5 us

profile of v1, /device:TPU:0, one launch (start us, length us, event | category | flops | bytes accessed | tf_op | source)
XLA Modules:
  0.0 313.8 jit_solution(3135774799250105685)
XLA Ops:
  0.6 104.2 %gather_and_attend.1 = (bf16[1536,2048]{1,0:T(8,128)(2,1)}, bf16[1536,1536]{1,0:T(8,128)(2,1)}, bf16[1536,2304]{1,0:T(8,128)(2,1)}, bf16[1024,1536]{1,0:T(8,128)...) custom-call(bf16[128,1536]{1,0:T(8,128)(2,1)} %bitcast.4, ...), custom_call_target="tpu_custom_call" | custom-call | tf_op jit(solution)/shard_map/gather_and_attend/pallas_call | solution.py:784
  104.9 195.3 %layer_back.1 = (bf16[128,1536]{1,0:T(8,128)(2,1)}, bf16[128,1536]{1,0:T(8,128)(2,1)}, bf16[4,8,48,2304]{3,2,1,0:T(8,128)(2,1)}, bf16[4,1152,384]{2,1,0:T(8,128)...) custom-call(bf16[128,1536]{1,0:T(8,128)(2,1)} %get-tuple-element.41.n_ref, ...), custom_call_target="tpu_custom_call" | custom-call | tf_op jit(solution)/shard_map/layer_back/pallas_call | solution.py:1511
  300.1 13.5 %widen.1 = (f32[192,8960]{1,0:T(8,128)}, f32[192,8960]{1,0:T(8,128)}, f32[1120,1536]{1,0:T(8,128)}, f32[192,2048]{1,0:T(8,128)}, f32[192,1536]{1,0:T(8,128)}, /*...) custom-call(bf16[4,8,48,2304]{3,2,1,0:T(8,128)(2,1)} %get-tuple-element.56.g_r, ...), custom_call_target="tpu_custom_call" | custom-call | tf_op jit(solution)/shard_map/widen/pallas_call | solution.py:1566
